TPU v7x, 32 devices: a whole 2x2x4 slice. The times are simulated.
32 devices in a mesh: section: 2 (over y), node: 4 (over z), local: 4 (over x, core).
Axes of the slice: x: 2, y: 2, z: 4, core: 2. Of those that a mesh axis runs over, the one named last changes fastest.
Arguments:
- prev_rows: bfloat16 [2, 2048, 3584], P('section', ('node', 'local')), may hold values from -6 to 6
- expert_ids: int32 [2, 2048, 1], P('section', ('node', 'local')), may hold values from 0 to 3; in each aligned block of 128 rows (0 to 127, 128 to 255, ..., all dimensions but the last counted through in order) at most 40 rows name the same one
- route_weight: float32 [2, 2048, 1], P('section', ('node', 'local')), may hold values from 0.3 to 1.5
- norm_gain: float32 [2, 3584], P('section'), may hold values from 0.1 to 1.9
- gate_weight: bfloat16 [2, 4, 3584, 1024], P('section', 'node', None, 'local'), may hold values from -0.09375 to 0.09375
- up_weight: bfloat16 [2, 4, 3584, 1024], P('section', 'node', None, 'local'), may hold values from -0.09375 to 0.09375
- down_weight: bfloat16 [2, 4, 1024, 3584], P('section', 'node', None, 'local'), may hold values from -0.1875 to 0.1875
Outputs:
- mixed: bfloat16 [2, 2048, 3584], P('section', ('node', 'local'))
Inputs may be any that keep to these rules, and one draw needn't show every extreme that they name: `expert_ids`: within the 128 tokens of one device no expert is named more than 40 times, and the rows of some device name some expert exactly 40 times.
All inputs are finite; a program needn't handle non-finite values.
Results may differ from a plain program's by a relative error of at most 0.0051.
Values may be sent and summed in bfloat16 or wider, within the bound.
A program may use at most 64 MiB of HBM per device.

v0:
```python
import jax
import jax.numpy as jnp
from jax import lax
from jax.sharding import PartitionSpec as P


def passed_along(value, axis, by):
    length = lax.axis_size(axis)
    return lax.ppermute(value, axis, [(i, (i + by) % length) for i in range(length)])


def per_device(prev_rows, expert_ids, route_weight, norm_gain, gate_weight, up_weight, down_weight):
    arrived_rows = passed_along(prev_rows, "section", 1)[0]
    tokens_dev = arrived_rows.shape[0]
    feature = arrived_rows.shape[1]
    choices_top = expert_ids.shape[2]
    experts = lax.axis_size("node")
    members = lax.axis_size("local")
    capacity = 5 * tokens_dev * choices_top // (4 * experts)
    slice_width = feature // members
    wide = arrived_rows.astype(jnp.float32)
    scale = lax.rsqrt(jnp.mean(wide * wide, axis=-1, keepdims=True) + 1e-06)
    normed = (wide * scale * norm_gain[0]).astype(jnp.bfloat16)
    flat_ids = expert_ids[0].reshape(-1)
    onehot = (flat_ids[:, None] == jnp.arange(experts, dtype=jnp.int32)[None, :]).astype(jnp.int32)
    slot = jnp.sum((jnp.cumsum(onehot, axis=0) - onehot) * onehot, axis=1)
    expert_axis = jnp.arange(experts, dtype=jnp.int32)[:, None, None]
    slot_axis = jnp.arange(capacity, dtype=jnp.int32)[None, :, None]
    selector = (
        (flat_ids[None, None, :] == expert_axis) & (slot[None, None, :] == slot_axis)
    ).astype(jnp.bfloat16)
    selector = selector.reshape(experts * capacity, tokens_dev * choices_top)
    repeated = jnp.repeat(normed, choices_top, axis=0)
    dispatched = jnp.dot(selector, repeated, preferred_element_type=jnp.float32).astype(
        jnp.bfloat16
    )
    dispatched = dispatched.reshape(experts, capacity, feature)
    w_gate = gate_weight[0, 0]
    w_up = up_weight[0, 0]
    w_down = down_weight[0, 0]
    landed = lax.all_to_all(dispatched, "node", split_axis=0, concat_axis=0, tiled=True)
    inputs = lax.all_gather(landed.reshape(-1, feature), "local", axis=0, tiled=True)
    gate = jnp.dot(inputs, w_gate, preferred_element_type=jnp.float32)
    upper = jnp.dot(inputs, w_up, preferred_element_type=jnp.float32)
    hidden = (jax.nn.silu(gate) * upper).astype(jnp.bfloat16)
    outputs = jnp.dot(
        lax.all_gather(hidden, "local", axis=1, tiled=True),
        w_down,
        preferred_element_type=jnp.float32,
    ).astype(jnp.bfloat16)
    arranged = outputs.reshape(members, experts, capacity, slice_width).transpose(1, 0, 2, 3)
    returned = lax.all_to_all(
        lax.all_to_all(arranged, "node", split_axis=0, concat_axis=0, tiled=True),
        "local",
        split_axis=1,
        concat_axis=3,
        tiled=True,
    )
    returned = returned.reshape(experts * capacity, feature)
    picked = jnp.einsum("ka,kd->ad", selector, returned, preferred_element_type=jnp.float32)
    picked = picked.reshape(tokens_dev, choices_top, feature)
    combined = jnp.sum(picked * route_weight[0][:, :, None], axis=1)
    return (wide + combined).astype(jnp.bfloat16)[None]


def solution(mesh):
    placed = (
        P("section", ("node", "local"), None),
        P("section", ("node", "local"), None),
        P("section", ("node", "local"), None),
        P("section", None),
        P("section", "node", None, "local"),
        P("section", "node", None, "local"),
        P("section", "node", None, "local"),
    )
    return jax.shard_map(
        per_device,
        mesh=mesh,
        in_specs=placed,
        out_specs=P("section", ("node", "local"), None),
        check_vma=False,
    )
```

profile of v0, /device:TPU:9, one launch (start us, length us, event | category | flops | bytes accessed | tf_op | source)
XLA Modules:
  0.0 183.8 jit_solution(402042521671097060)
XLA Ops:
  6.5 0.0 copy-start
  6.5 0.0 all-gather.3.cloned.1.call-start
  6.5 1.2 collective-permute-start
  7.8 0.8 reduce.1
  8.5 0.7 fusion.25
  9.3 0.2 reduce_window_sum.11
  9.5 0.8 select_reduce_fusion
  10.3 0.7 iota_compare_fusion.2
  11.0 17.0 %collective-permute-done = bf16[1,128,3584]{2,1,0:T(8,128)(2,1)S(1)} collective-permute-done((bf16[1,128,3584]{2,1,0:T(8,128)(2,1)}, bf16[1,128,3584]{2,1,0:T(8,128)(2,1)S(1)}, u32[]{:S(2)}, u32[]{:S(2)}) %collective-permute-start) | collective-permute-done | bytes 917536 | tf_op jit(solution)/shard_map/ppermute | solution.py:9
  28.0 0.3 fusion.3
  28.2 0.5 convolution_convert_fusion
  28.8 30.0 %all_to_all.25 = bf16[4,40,3584]{2,1,0:T(8,128)(2,1)} all-to-all(bf16[4,40,3584]{2,1,0:T(8,128)(2,1)S(1)} %bitcast.48), channel_id=1, replica_groups=mesh['section'=2,'node'=4,'local'=4] {'node'}, dimensions={0} | all-to-all | bytes 2293760 | tf_op jit(solution)/shard_map/all_to_all | solution.py:41
  58.8 0.0 all-gather.3.cloned.1.call-update
  58.9 0.0 all-gather.5.cloned.1.call-start
  58.9 38.8 %all-gather.3.cloned.1.call-done = bf16[640,3584]{1,0:T(8,128)(2,1)} async-done(((bf16[160,3584]{1,0:T(8,128)(2,1)}), bf16[640,3584]{1,0:T(8,128)(2,1)}) %all-gather.3.cloned.1.call-update) | async-done | bytes 4587536 | tf_op jit(solution)/shard_map/all_gather | solution.py:42
  97.7 0.0 copy-start.2
  97.7 0.0 copy-start.3
  97.7 4.4 %fusion.10 = f32[640,256]{1,0:T(8,128)S(1)} fusion(bf16[640,3584]{1,0:T(8,128)(2,1)} %all-gather.3.cloned.1.call-done, bf16[1,1,3584,256]{3,2,1,0:T(8,128)(2,1)} %param.11), kind=kOutput, calls=%fused_computation.14 | convolution fusion | flops 1174405120 | bytes 7077888 | tf_op jit(solution)/shard_map/dot_general | solution.py:43
  102.1 0.0 copy-done.2
  102.1 0.4 copy-done.3
  102.5 2.1 %fusion.18 = bf16[640,256]{1,0:T(8,128)(2,1)} fusion(bf16[640,3584]{1,0:T(8,128)(2,1)S(1)} %copy-done.2, bf16[1,1,3584,256]{3,2,1,0:T(8,128)(2,1)S(1)} %copy-done.3, f32[640,256]{1,0:T(8,128)S(1)} %fusion.10), kind=kOutput, calls=%fused_computation.18 | convolution fusion | flops 1175388160 | bytes 7405568 | tf_op jit(solution)/shard_map/dot_general | solution.py:44
  104.6 0.0 all-gather.5.cloned.1.call-update
  104.6 18.5 %all-gather.5.cloned.1.call-done = bf16[640,1024]{1,0:T(8,128)(2,1)} async-done(((bf16[640,256]{1,0:T(8,128)(2,1)}), bf16[640,1024]{1,0:T(8,128)(2,1)}) %all-gather.5.cloned.1.call-update) | async-done | bytes 1310736 | tf_op jit(solution)/shard_map/all_gather | solution.py:47
  123.1 0.0 copy-done
  123.1 2.8 %fusion.12 = bf16[640,896]{1,0:T(8,128)(2,1)S(1)} fusion(bf16[640,1024]{1,0:T(8,128)(2,1)} %all-gather.5.cloned.1.call-done, bf16[1,1,1024,896]{3,2,1,0:T(8,128)(2,1)S(1)} %copy-done), kind=kOutput, calls=%fused_computation.16 | convolution fusion | flops 1174978560 | bytes 4292608 | tf_op jit(solution)/shard_map/dot_general | solution.py:46
  126.0 0.1 copy.15
  126.1 29.8 %all_to_all.26 = bf16[4,4,40,896]{3,2,1,0:T(8,128)(2,1)S(1)} all-to-all(bf16[4,4,40,896]{3,2,1,0:T(8,128)(2,1)S(1)} %bitcast.49), channel_id=1, replica_groups=mesh['section'=2,'node'=4,'local'=4] {'node'}, dimensions={0} | all-to-all | bytes 2293760 | tf_op jit(solution)/shard_map/all_to_all | solution.py:53
  155.9 0.1 copy.11
  156.0 18.9 %all_to_all.27 = bf16[4,4,40,896]{3,2,0,1:T(8,128)(2,1)S(1)} all-to-all(bf16[4,4,40,896]{3,2,0,1:T(8,128)(2,1)S(1)} %copy.11), channel_id=1, replica_groups=mesh['section'=2,'node'=4,'local'=4] {'local'}, dimensions={1} | all-to-all | bytes 2293760 | tf_op jit(solution)/shard_map/all_to_all | solution.py:52
  174.9 0.0 copy-start.1
  174.9 0.6 copy.12
  175.5 0.1 copy.13
  175.6 0.0 copy-done.1
  175.6 1.4 fusion.2
  (3 shorter events, 0.0 us)
Async XLA Ops:
  6.5 116.6 %copy-start = (bf16[1,1,1024,896]{3,2,1,0:T(8,128)(2,1)S(1)}, bf16[1,1,1024,896]{3,2,1,0:T(8,128)(2,1)}, u32[]{:S(2)}) copy-start(bf16[1,1,1024,896]{3,2,1,0:T(8,128)(2,1)} %param.13) | copy-start | bytes 5505028
  6.5 91.2 %all-gather.3.cloned.1.call-start = ((), (), s32[]{:S(2)}) async-start(), calls=%async_computation.3 | async-start | bytes 5734400 | tf_op jit(solution)/shard_map/all_gather | solution.py:42
  6.5 21.4 %collective-permute-start = (bf16[1,128,3584]{2,1,0:T(8,128)(2,1)}, bf16[1,128,3584]{2,1,0:T(8,128)(2,1)S(1)}, u32[]{:S(2)}, u32[]{:S(2)}) collective-permute-start(bf16[1,128,3584]{2,1,0:T(8,128)(2,1)} %param.7), channel_id=1, source_target_pairs={{0,16},{16,0},{1,17},{17,1},{2,18},{18,2},{3,19},{19,3},{4,20},{20... | collective-permute-start | bytes 2752520 | tf_op jit(solution)/shard_map/ppermute | solution.py:9
  58.9 64.3 %all-gather.5.cloned.1.call-start = ((), (), s32[]{:S(2)}) async-start(), calls=%async_computation.4 | async-start | bytes 1638400 | tf_op jit(solution)/shard_map/all_gather | solution.py:47
  97.7 4.4 %copy-start.2 = (bf16[640,3584]{1,0:T(8,128)(2,1)S(1)}, bf16[640,3584]{1,0:T(8,128)(2,1)}, u32[]{:S(2)}) copy-start(bf16[640,3584]{1,0:T(8,128)(2,1)} %all-gather.3.cloned.1.call-done) | copy-start | bytes 13762564
  97.7 4.8 %copy-start.3 = (bf16[1,1,3584,256]{3,2,1,0:T(8,128)(2,1)S(1)}, bf16[1,1,3584,256]{3,2,1,0:T(8,128)(2,1)}, u32[]{:S(2)}) copy-start(bf16[1,1,3584,256]{3,2,1,0:T(8,128)(2,1)} %param.12) | copy-start | bytes 5505028
  174.9 0.7 copy-start.1
Sparse Core Ops, SparseCore 0:
  59.0 38.7 all-gather.2
  104.8 18.3 all-gather.4
where the time goes:
time: 187 us; the launch traced here: 184 us
  blocking collectives  78.7 us (42%)
  waiting for transfers between devices  74.4 us (40%)
  between operations  13.5 us (7%)
  matrix products  11.2 us (6%)
  other arithmetic  3.46 us (2%)
    all_gather x1, waiting for transfers between devices, per_device(): lax.all_gather(landed.reshape(-1, feature), 'local', axis=0, tiled=True)  38.8 us
    all_to_all x1, blocking collectives, per_device(): lax.all_to_all(dispatched, 'node', split_axis=0, concat_axis=0, tiled=True)  30 us
    all_to_all x1, blocking collectives, per_device(): lax.all_to_all(arranged, 'node', split_axis=0, concat_axis=0, tiled=True)  29.8 us
    all_to_all x1, blocking collectives, per_device(): lax.all_to_all(lax.all_to_all(arranged, 'node', split_axis=0, concat_axis...  18.9 us
    all_gather x1, waiting for transfers between devices, per_device(): lax.all_gather(hidden, 'local', axis=1, tiled=True)  18.5 us
    ppermute x1, waiting for transfers between devices, passed_along(): lax.ppermute(value, axis, [(i, (i + by) % length) for i in range(length)])  17 us
    dot_general x1, matrix products, per_device(): gate = jnp.dot(inputs, w_gate, preferred_element_type=jnp.float32)  4.37 us
  transfers between devices with their start and end apart: 3, of which 3 were waited for; matrix products, arithmetic and copies ran while one was open for 2% of the time, Pallas kernels for 0%

commit v1 on v0

v1 whole, which is shorter than its diff:
```python
import functools

import jax
import jax.numpy as jnp
from jax import lax
from jax.experimental import pallas as pl
from jax.experimental.pallas import tpu as pltpu
from jax.sharding import PartitionSpec as P

MESH = pl.DeviceIdType.MESH
HALVES = 2
CHUNK = 512


def kernel(
    sections, experts, members, slots,
    prev, ids, weight, gain, w_gate, w_up, w_down, out,
    rows, scale_out, scale_in, sel, sel_t, packed, arrived, w_in, w_out, total, hidden, results, returned,
    w_sem, y_send, y_recv, z_send, z_recv, g_send, g_recv, f_send, f_recv,
    h_send, h_recv, k_send, k_recv, r_send, r_recv,
):
    s, n, l = lax.axis_index("section"), lax.axis_index("node"), lax.axis_index("local")
    tokens, feature = prev.shape
    chunks = feature // CHUNK
    part = CHUNK // HALVES
    units = w_gate.shape[1]
    width = w_down.shape[1]
    tiles = -(-width // 128)
    ends = [min(128, width - 128 * t) for t in range(tiles)]
    group = members * slots
    chips = members // 2
    sibling = l + 1 - 2 * lax.rem(l, 2)
    order = sorted(range(experts), key=lambda k: -min(k, experts - k))

    loads = [
        pltpu.make_async_copy(w_gate, w_in.at[:, pl.ds(0, units)], w_sem.at[0]),
        pltpu.make_async_copy(w_up, w_in.at[:, pl.ds(units, units)], w_sem.at[1]),
        pltpu.make_async_copy(w_down, w_out, w_sem.at[2]),
    ]
    for load in loads:
        load.start()

    barrier = pltpu.get_barrier_semaphore()
    after, before = lax.rem(s + 1, sections), lax.rem(s + sections - 1, sections)
    for other in (after, before):
        pl.semaphore_signal(barrier, inc=1, device_id={"section": other, "node": n, "local": l}, device_id_type=MESH)
    for k in range(experts):
        for m in range(members):
            if k or m:
                place = {"section": s, "node": lax.rem(n + k, experts), "local": lax.rem(l + m, members)}
                pl.semaphore_signal(barrier, inc=1, device_id=place, device_id_type=MESH)

    wide = prev[...].astype(jnp.float32)
    mean = jnp.sum(wide * wide, axis=1, keepdims=True) / feature
    scale_out[...] = jnp.broadcast_to(lax.rsqrt(mean + 1e-06), scale_out.shape)

    chosen = ids[...]
    lanes = lax.broadcasted_iota(jnp.int32, (tokens, 128), 1)
    onehot = jnp.where(chosen == lanes, 1.0, 0.0)
    earlier = lax.broadcasted_iota(jnp.int32, (tokens, tokens), 1) < lax.broadcasted_iota(jnp.int32, (tokens, tokens), 0)
    counts = jnp.dot(
        jnp.where(earlier, 1.0, 0.0).astype(jnp.bfloat16), onehot.astype(jnp.bfloat16),
        preferred_element_type=jnp.float32,
    )
    slot = jnp.sum(counts * onehot, axis=1, keepdims=True)
    target = chosen.astype(jnp.float32) * slots + slot
    places = lax.broadcasted_iota(jnp.int32, (tokens, sel.shape[0]), 1).astype(jnp.float32)
    spread = jnp.where(target == places, 1.0, 0.0)
    sel_t[...] = spread.astype(jnp.bfloat16)
    sel[...] = spread.T.astype(jnp.bfloat16)
    total[...] = jnp.zeros_like(total)

    pl.semaphore_wait(barrier, experts * members + 1)

    def remote(src, dst, send, recv, **place):
        where = {"section": s, "node": n, "local": l}
        where.update(place)
        return pltpu.make_async_remote_copy(
            src_ref=src, dst_ref=dst, send_sem=send, recv_sem=recv, device_id=where, device_id_type=MESH
        )

    def columns(c):
        return pl.ds(pl.multiple_of(c * CHUNK, CHUNK), CHUNK)

    def scale_copy():
        return remote(scale_out, scale_in, y_send.at[chunks], y_recv.at[chunks], section=after)

    def y_copy(c):
        return remote(prev.at[:, columns(c)], rows.at[:, columns(c)], y_send.at[c], y_recv.at[c], section=after)

    def z_copy(c, k):
        node = lax.rem(n + k, experts)
        if k == 0:
            return pltpu.make_async_copy(packed.at[c, n], arrived.at[c, n, l], z_recv.at[c, 0])
        return remote(packed.at[c, node], arrived.at[c, n, l], z_send.at[c, k], z_recv.at[c, k], node=node)

    def g_copy(c, m):
        block = arrived.at[c, :, l]
        peer = sibling if m == 0 else lax.rem(l + 2 * m, members)
        return remote(block, block, g_send.at[c, m], g_recv.at[c, m], local=peer)

    def f_copy(c, m):
        block = arrived.at[c, :, lax.rem(l + members - 2 * m, members)]
        return remote(block, block, f_send.at[c, m], f_recv.at[c, m], local=sibling)

    def h_copy(k, m):
        block = hidden.at[lax.rem(n + k, experts), l]
        peer = sibling if m == 0 else lax.rem(l + 2 * m, members)
        return remote(block, block, h_send.at[k, m], h_recv.at[k, m], local=peer)

    def k_copy(k, m):
        block = hidden.at[lax.rem(n + k, experts), lax.rem(l + members - 2 * m, members)]
        return remote(block, block, k_send.at[k, m], k_recv.at[k, m], local=sibling)

    def r_copy(k, m):
        node, local = lax.rem(n + k, experts), lax.rem(l + m, members)
        if k == 0 and m == 0:
            return pltpu.make_async_copy(results.at[n, l], returned.at[n, l], r_recv.at[0, 0])
        return remote(
            results.at[node, local], returned.at[n, l], r_send.at[k, m], r_recv.at[k, m], node=node, local=local
        )

    scale_copy().start()

    @pl.loop(0, chunks)
    def _(c):
        y_copy(c).start()

    scale_copy().wait_recv()

    @pl.loop(0, chunks + 3)
    def _(step):
        @pl.when(step < chunks)
        def _():
            c = step
            y_copy(c).wait_recv()
            normed = (rows[:, columns(c)].astype(jnp.float32) * scale_in[:, 0:1] * gain[:, columns(c)]).astype(jnp.bfloat16)
            placed = jnp.dot(sel[0 : experts * slots, :], normed, preferred_element_type=jnp.float32)
            for e in range(experts):
                for half in range(HALVES):
                    packed[c, e, half * slots : (half + 1) * slots, :] = placed[
                        e * slots : (e + 1) * slots, half * part : (half + 1) * part
                    ].astype(jnp.bfloat16)
            for k in order:
                z_copy(c, k).start()

        @pl.when(jnp.logical_and(step >= 1, step < chunks + 1))
        def _():
            c = step - 1
            z_copy(c, 0).wait()
            for k in range(1, experts):
                z_copy(c, k).wait_recv()
            for m in list(range(1, chips)) + [0]:
                g_copy(c, m).start()

        @pl.when(jnp.logical_and(step >= 2, step < chunks + 2))
        def _():
            c = step - 2
            for m in range(1, chips):
                g_copy(c, m).wait_recv()
                f_copy(c, m).start()

        @pl.when(step >= 3)
        def _():
            c = step - 3

            @pl.when(c == 0)
            def _():
                for load in loads:
                    load.wait()

            g_copy(c, 0).wait_recv()
            for m in range(1, chips):
                f_copy(c, m).wait_recv()
            sides = [
                arrived[c, :, :, half * slots : (half + 1) * slots, :]
                .astype(jnp.float32).reshape(experts * group, part).astype(jnp.bfloat16)
                for half in range(HALVES)
            ]
            total[...] += jnp.dot(
                jnp.concatenate(sides, axis=1), w_in[columns(c), :], preferred_element_type=jnp.float32
            )

    for k in order:
        node = lax.rem(n + k, experts)
        span = pl.ds(pl.multiple_of(node * group, 16), group)
        gate, upper = total[span, 0:units], total[span, units : 2 * units]
        hidden[node, l] = (gate / (1.0 + jnp.exp(-gate)) * upper).astype(jnp.bfloat16)
        for m in list(range(1, chips)) + [0]:
            h_copy(k, m).start()

    for k in order:
        node = lax.rem(n + k, experts)
        for m in range(1, chips):
            h_copy(k, m).wait_recv()
            k_copy(k, m).start()
        h_copy(k, 0).wait_recv()
        for m in range(1, chips):
            k_copy(k, m).wait_recv()
        inner = jnp.concatenate([hidden[node, j] for j in range(members)], axis=1)
        made = jnp.dot(inner, w_out[...], preferred_element_type=jnp.float32)
        for j in range(members):
            for t in range(tiles):
                results[node, j, t * slots : (t + 1) * slots, 0 : ends[t]] = made[
                    j * slots : (j + 1) * slots, t * 128 : t * 128 + ends[t]
                ].astype(jnp.bfloat16)
        for m in range(members):
            r_copy(k, m).start()

    for k in order:
        for m in range(members):
            if k == 0 and m == 0:
                r_copy(k, m).wait()
            else:
                r_copy(k, m).wait_recv()

    for j in range(members):
        table = jnp.concatenate(
            [
                jnp.concatenate(
                    [returned[e, j, t * slots : (t + 1) * slots, 0 : ends[t]].astype(jnp.float32) for t in range(tiles)],
                    axis=1,
                )
                for e in range(experts)
            ],
            axis=0,
        ).astype(jnp.bfloat16)
        picked = jnp.dot(sel_t[:, 0 : experts * slots], table, preferred_element_type=jnp.float32)
        span = slice(j * width, (j + 1) * width)
        out[:, span] = (rows[:, span].astype(jnp.float32) + picked * weight[...]).astype(jnp.bfloat16)

    scale_copy().wait_send()

    @pl.loop(0, chunks)
    def _(c):
        y_copy(c).wait_send()
        for k in range(1, experts):
            z_copy(c, k).wait_send()
        for m in range(chips):
            g_copy(c, m).wait_send()
        for m in range(1, chips):
            f_copy(c, m).wait_send()

    for k in range(experts):
        for m in range(chips):
            h_copy(k, m).wait_send()
        for m in range(1, chips):
            k_copy(k, m).wait_send()
        for m in range(members):
            if k or m:
                r_copy(k, m).wait_send()


def per_device(sections, experts, members, prev_rows, expert_ids, route_weight, norm_gain, gate_weight, up_weight, down_weight):
    prev = prev_rows[0]
    tokens, feature = prev.shape
    capacity = 5 * tokens * expert_ids.shape[2] // (4 * experts)
    slots = -(-capacity // 8) * 8
    units, width = gate_weight.shape[3], down_weight.shape[3]
    chunks, chips = feature // CHUNK, members // 2
    lines = -(-(-(-width // 128) * slots) // 16) * 16
    group = members * slots
    padded = -(-(experts * slots) // 128) * 128
    bf16, f32 = jnp.bfloat16, jnp.float32
    dma = pltpu.SemaphoreType.DMA
    vmem, anywhere = pl.BlockSpec(memory_space=pltpu.VMEM), pl.BlockSpec(memory_space=pl.ANY)
    mixed = pl.pallas_call(
        functools.partial(kernel, sections, experts, members, slots),
        out_shape=jax.ShapeDtypeStruct((tokens, feature), bf16),
        in_specs=[vmem] * 4 + [anywhere] * 3,
        out_specs=vmem,
        scratch_shapes=[
            pltpu.VMEM((tokens, feature), bf16),
            pltpu.VMEM((tokens, 128), f32),
            pltpu.VMEM((tokens, 128), f32),
            pltpu.VMEM((padded, tokens), bf16),
            pltpu.VMEM((tokens, padded), bf16),
            pltpu.VMEM((chunks, experts, HALVES * slots, CHUNK // HALVES), bf16),
            pltpu.VMEM((chunks, experts, members, HALVES * slots, CHUNK // HALVES), bf16),
            pltpu.VMEM((feature, 2 * units), bf16),
            pltpu.VMEM((members * units, width), bf16),
            pltpu.VMEM((experts * group, 2 * units), f32),
            pltpu.VMEM((experts, members, group, units), bf16),
            pltpu.VMEM((experts, members, lines, 128), bf16),
            pltpu.VMEM((experts, members, lines, 128), bf16),
            dma((3,)),
            dma((chunks + 1,)), dma((chunks + 1,)),
            dma((chunks, experts)), dma((chunks, experts)),
            dma((chunks, chips)), dma((chunks, chips)),
            dma((chunks, chips)), dma((chunks, chips)),
            dma((experts, chips)), dma((experts, chips)),
            dma((experts, chips)), dma((experts, chips)),
            dma((experts, members)), dma((experts, members)),
        ],
        compiler_params=pltpu.CompilerParams(
            collective_id=0, has_side_effects=True, vmem_limit_bytes=56 * 1024 * 1024
        ),
    )(prev, expert_ids[0], route_weight[0], norm_gain, gate_weight[0, 0], up_weight[0, 0], down_weight[0, 0])
    return mixed[None]


def solution(mesh):
    placed = (
        P("section", ("node", "local"), None),
        P("section", ("node", "local"), None),
        P("section", ("node", "local"), None),
        P("section", None),
        P("section", "node", None, "local"),
        P("section", "node", None, "local"),
        P("section", "node", None, "local"),
    )
    sizes = mesh.shape
    return jax.shard_map(
        functools.partial(per_device, sizes["section"], sizes["node"], sizes["local"]),
        mesh=mesh,
        in_specs=placed,
        out_specs=P("section", ("node", "local"), None),
        check_vma=False,
    )
```

time: 187 us -> 88.6 us (0.47); the launches traced: 184 us -> 88.4 us
  Pallas kernels: 0 us -> 83.5 us
  blocking collectives: 78.7 us -> 0 us
  waiting for transfers between devices: 74.4 us -> 0 us
  between operations: 13.5 us -> 0.01 us
  matrix products: 11.2 us -> 0 us
  local copies, waits for them, and re-layouts: 1.32 us -> 4.93 us
  other arithmetic: 3.46 us -> 0 us
    pallas_call x0 -> x1, Pallas kernels: none -> 83.5 us  [per_device(): pl.pallas_call(functools.partial(kernel, sections, experts, members, slot...]
    all_to_all x3 -> x0, blocking collectives: 78.7 us -> none  [the longest x1 30 us: per_device(): lax.all_to_all(dispatched, 'node', split_axis=0, concat_axis=0, tiled=True)]
    all_gather x2 -> x0, waiting for transfers between devices: 57.3 us -> none  [the longest x1 38.8 us: per_device(): lax.all_gather(landed.reshape(-1, feature), 'local', axis=0, tiled=True)]
    ppermute x1 -> x0, waiting for transfers between devices: 17 us -> none  [passed_along(): lax.ppermute(value, axis, [(i, (i + by) % length) for i in range(length)])]
    dot_general x5 -> x0, matrix products: 11.2 us -> none  [the longest x1 4.37 us: per_device(): gate = jnp.dot(inputs, w_gate, preferred_element_type=jnp.float32)]
    squeeze x0 -> x2, local copies, waits for them, and re-layouts: none -> 2.77 us  [the longest x1 1.39 us: per_device(): expert_ids[0]]
  transfers between devices with their start and end apart: 3 -> 0, of which waited for: 3 -> 0; matrix products, arithmetic and copies ran while one was open for 2% -> 0% of each run, Pallas kernels for 0% -> 0%
where the time goes in v1:
time: 88.6 us; the launch traced here: 88.4 us
  Pallas kernels  83.5 us (94%)
  local copies, waits for them, and re-layouts  4.93 us (6%)
    pallas_call x1, Pallas kernels, per_device(): pl.pallas_call(functools.partial(kernel, sections, experts, members, slot...  83.5 us
    unnamed x1, local copies, waits for them, and re-layouts  2.16 us

profile of v1, /device:TPU:9, one launch (start us, length us, event | category | flops | bytes accessed | tf_op | source)
XLA Modules:
  0.0 88.4 jit_solution(11695272169737278658)
XLA Ops:
  0.0 1.4 %copy.8.ids = s32[128,1]{1,0:T(8,128)} copy(s32[128,1]{0,1:T(1,128)} %bitcast.12) | data formatting | bytes 1024 | tf_op jit(solution)/shard_map/squeeze | solution.py:298
  1.4 1.4 %copy.9.weight = f32[128,1]{1,0:T(8,128)} copy(f32[128,1]{0,1:T(1,128)} %bitcast.13) | data formatting | bytes 1024 | tf_op jit(solution)/shard_map/squeeze | solution.py:298
  2.8 83.5 %shard_map.73 = bf16[128,3584]{1,0:T(8,128)(2,1)} custom-call(bf16[128,3584]{1,0:T(8,128)(2,1)} %bitcast.11, s32[128,1]{1,0:T(8,128)} %copy.8.ids, f32[128,1]{1,0:T(8,128)} %copy.9.weight, f32[1,3584]{1,0:T(1,128)} %gain.1, bf16[3584,256]{1,0:T(8,128)(2,1)} %bitcast.8, bf16[3584,256]{1,0:T(8,128)(2,1)} %bitcast.9, bf16[1024,896]{1,0:T(8,128)(2,1)} %bitcast.10), custom_call_target="tpu_custom_call" | custom-call | tf_op jit(solution)/shard_map/pallas_call | solution.py:267
  86.2 2.2 %copy.11 = bf16[1,128,3584]{2,1,0:T(8,128)(2,1)} copy(bf16[1,128,3584]{2,1,0:T(8,128)(2,1)} %bitcast.7) | data formatting | bytes 1835008

commit v2 on v0

v2 whole, which is shorter than its diff:
```python
import functools

import jax
import jax.numpy as jnp
from jax import lax
from jax.experimental import pallas as pl
from jax.experimental.pallas import tpu as pltpu
from jax.sharding import PartitionSpec as P

MESH = pl.DeviceIdType.MESH
HALVES = 2
CHUNK = 512
LAG = 3


def split(slots):
    first = 8 * -(-slots // 16)
    return (first, slots - first)


def kernel(sections, experts, members, slots, prev, ids, weight, gain, w_gate, w_up, w_down, out, *scratch):
    rows, normal, scale_out, scale_in, scale, mid, w_in, w_out, w_sem, y_send, y_recv = scratch[:11]
    own = (len(scratch) - 11) // 2
    parts = [scratch[11 : 11 + own], scratch[11 + own :]]
    s, n, l = lax.axis_index("section"), lax.axis_index("node"), lax.axis_index("local")
    tokens, feature = prev.shape
    chunks = feature // CHUNK
    part = CHUNK // HALVES
    units = w_gate.shape[1]
    width = w_down.shape[1]
    tiles = -(-width // 128)
    ends = [min(128, width - 128 * t) for t in range(tiles)]
    chips = members // 2
    sibling = l + 1 - 2 * lax.rem(l, 2)
    order = sorted(range(experts), key=lambda k: -min(k, experts - k))

    loads = [
        pltpu.make_async_copy(w_gate, w_in.at[:, pl.ds(0, units)], w_sem.at[0]),
        pltpu.make_async_copy(w_up, w_in.at[:, pl.ds(units, units)], w_sem.at[1]),
        pltpu.make_async_copy(w_down, w_out, w_sem.at[2]),
    ]
    for load in loads:
        load.start()

    barrier = pltpu.get_barrier_semaphore()
    after, before = lax.rem(s + 1, sections), lax.rem(s + sections - 1, sections)
    for other in (after, before):
        pl.semaphore_signal(barrier, inc=1, device_id={"section": other, "node": n, "local": l}, device_id_type=MESH)
    for k in range(experts):
        for m in range(members):
            if k or m:
                place = {"section": s, "node": lax.rem(n + k, experts), "local": lax.rem(l + m, members)}
                pl.semaphore_signal(barrier, inc=1, device_id=place, device_id_type=MESH)

    wide = prev[...].astype(jnp.float32)
    mean = jnp.sum(wide * wide, axis=1, keepdims=True) / feature
    scale_out[...] = jnp.broadcast_to(lax.rsqrt(mean + 1e-06), (tokens, 128)).T[0:8, :]

    chosen = jnp.broadcast_to(ids[...].astype(jnp.float32), (128, tokens)).T
    lanes = lax.broadcasted_iota(jnp.int32, (tokens, 128), 1).astype(jnp.float32)
    onehot = jnp.where(chosen == lanes, 1.0, 0.0)
    earlier = lax.broadcasted_iota(jnp.int32, (tokens, tokens), 1) < lax.broadcasted_iota(jnp.int32, (tokens, tokens), 0)
    counts = jnp.dot(
        jnp.where(earlier, 1.0, 0.0).astype(jnp.bfloat16), onehot.astype(jnp.bfloat16),
        preferred_element_type=jnp.float32,
    )
    slot = jnp.sum(counts * onehot, axis=1, keepdims=True)
    pool = split(slots)
    for p in range(2):
        sel, sel_t, total = parts[p][0], parts[p][1], parts[p][4]
        local_slot = slot - (pool[0] if p else 0)
        inside = jnp.logical_and(local_slot >= 0, local_slot < pool[p])
        target = jnp.where(inside, chosen[:, 0:1] * pool[p] + local_slot, -1.0)
        places = lax.broadcasted_iota(jnp.int32, (tokens, sel.shape[0]), 1).astype(jnp.float32)
        spread = jnp.where(target == places, 1.0, 0.0)
        sel_t[...] = spread.astype(jnp.bfloat16)
        sel[...] = spread.T.astype(jnp.bfloat16)
        total[...] = jnp.zeros_like(total)
    factor = jnp.broadcast_to(weight[...], (128, tokens)).T[:, 0:1]

    pl.semaphore_wait(barrier, experts * members + 1)

    def remote(src, dst, send, recv, **place):
        where = {"section": s, "node": n, "local": l}
        where.update(place)
        return pltpu.make_async_remote_copy(
            src_ref=src, dst_ref=dst, send_sem=send, recv_sem=recv, device_id=where, device_id_type=MESH
        )

    def columns(c):
        return pl.ds(pl.multiple_of(c * CHUNK, CHUNK), CHUNK)

    def scale_copy():
        return remote(scale_out, scale_in, y_send.at[chunks], y_recv.at[chunks], section=after)

    def y_copy(c):
        return remote(prev.at[:, columns(c)], rows.at[:, columns(c)], y_send.at[c], y_recv.at[c], section=after)

    class Part:
        def __init__(self, p):
            self.p, self.slots, self.group = p, pool[p], members * pool[p]
            (self.sel, self.sel_t, self.packed, self.arrived, self.total, self.hidden, self.results, self.returned,
             self.z_send, self.z_recv, self.g_send, self.g_recv, self.f_send, self.f_recv,
             self.h_send, self.h_recv, self.k_send, self.k_recv, self.r_send, self.r_recv) = parts[p]

        def z_copy(self, c, k):
            node = lax.rem(n + k, experts)
            if k == 0:
                return pltpu.make_async_copy(self.packed.at[c, n], self.arrived.at[c, n, l], self.z_recv.at[c, 0])
            return remote(
                self.packed.at[c, node], self.arrived.at[c, n, l], self.z_send.at[c, k], self.z_recv.at[c, k], node=node
            )

        def g_copy(self, c, m):
            block = self.arrived.at[c, :, l]
            peer = sibling if m == 0 else lax.rem(l + 2 * m, members)
            return remote(block, block, self.g_send.at[c, m], self.g_recv.at[c, m], local=peer)

        def f_copy(self, c, m):
            block = self.arrived.at[c, :, lax.rem(l + members - 2 * m, members)]
            return remote(block, block, self.f_send.at[c, m], self.f_recv.at[c, m], local=sibling)

        def h_copy(self, k, m):
            block = self.hidden.at[lax.rem(n + k, experts), l]
            peer = sibling if m == 0 else lax.rem(l + 2 * m, members)
            return remote(block, block, self.h_send.at[k, m], self.h_recv.at[k, m], local=peer)

        def k_copy(self, k, m):
            block = self.hidden.at[lax.rem(n + k, experts), lax.rem(l + members - 2 * m, members)]
            return remote(block, block, self.k_send.at[k, m], self.k_recv.at[k, m], local=sibling)

        def r_copy(self, k, m):
            node, local = lax.rem(n + k, experts), lax.rem(l + m, members)
            if k == 0 and m == 0:
                return pltpu.make_async_copy(self.results.at[n, l], self.returned.at[n, l], self.r_recv.at[0, 0])
            return remote(
                self.results.at[node, local], self.returned.at[n, l], self.r_send.at[k, m], self.r_recv.at[k, m],
                node=node, local=local,
            )

        def dispatch(self, c):
            if self.p == 0:
                y_copy(c).wait_recv()
                normed = (
                    rows[:, columns(c)].astype(jnp.float32) * scale[:, 0:1] * gain[:, columns(c)]
                ).astype(jnp.bfloat16)
                normal[:, columns(c)] = normed
            else:
                normed = normal[:, columns(c)]
            placed = jnp.dot(
                self.sel[0 : experts * self.slots, :], normed, preferred_element_type=jnp.float32
            )
            for e in range(experts):
                for half in range(HALVES):
                    self.packed[c, e, half * self.slots : (half + 1) * self.slots, :] = placed[
                        e * self.slots : (e + 1) * self.slots, half * part : (half + 1) * part
                    ].astype(jnp.bfloat16)
            for k in order:
                self.z_copy(c, k).start()

        def share(self, c):
            self.z_copy(c, 0).wait()
            for k in range(1, experts):
                self.z_copy(c, k).wait_recv()
            for m in list(range(1, chips)) + [0]:
                self.g_copy(c, m).start()

        def hand_on(self, c):
            for m in range(1, chips):
                self.g_copy(c, m).wait_recv()
                self.f_copy(c, m).start()

        def multiply(self, c):
            self.g_copy(c, 0).wait_recv()
            for m in range(1, chips):
                self.f_copy(c, m).wait_recv()
            sides = [
                self.arrived[c, :, :, half * self.slots : (half + 1) * self.slots, :]
                .astype(jnp.float32).reshape(experts * self.group, part).astype(jnp.bfloat16)
                for half in range(HALVES)
            ]
            self.total[...] += jnp.dot(
                jnp.concatenate(sides, axis=1), w_in[columns(c), :], preferred_element_type=jnp.float32
            )

        def activate(self):
            for k in order:
                node = lax.rem(n + k, experts)
                span = pl.ds(pl.multiple_of(node * self.group, 16), self.group)
                gate, upper = self.total[span, 0:units], self.total[span, units : 2 * units]
                self.hidden[node, l] = (gate / (1.0 + jnp.exp(-gate)) * upper).astype(jnp.bfloat16)
                for m in list(range(1, chips)) + [0]:
                    self.h_copy(k, m).start()

        def give_back(self):
            for k in order:
                node = lax.rem(n + k, experts)
                for m in range(1, chips):
                    self.h_copy(k, m).wait_recv()
                    self.k_copy(k, m).start()
                self.h_copy(k, 0).wait_recv()
                for m in range(1, chips):
                    self.k_copy(k, m).wait_recv()
                inner = jnp.concatenate([self.hidden[node, j] for j in range(members)], axis=1)
                made = jnp.dot(inner, w_out[...], preferred_element_type=jnp.float32)
                for j in range(members):
                    for t in range(tiles):
                        self.results[node, j, t * self.slots : (t + 1) * self.slots, 0 : ends[t]] = made[
                            j * self.slots : (j + 1) * self.slots, t * 128 : t * 128 + ends[t]
                        ].astype(jnp.bfloat16)
                for m in range(members):
                    self.r_copy(k, m).start()

        def collect(self):
            for k in order:
                for m in range(members):
                    if k == 0 and m == 0:
                        self.r_copy(k, m).wait()
                    else:
                        self.r_copy(k, m).wait_recv()

        def picked(self, j):
            table = jnp.concatenate(
                [
                    jnp.concatenate(
                        [
                            self.returned[e, j, t * self.slots : (t + 1) * self.slots, 0 : ends[t]].astype(jnp.float32)
                            for t in range(tiles)
                        ],
                        axis=1,
                    )
                    for e in range(experts)
                ],
                axis=0,
            ).astype(jnp.bfloat16)
            return jnp.dot(self.sel_t[:, 0 : experts * self.slots], table, preferred_element_type=jnp.float32)

        def settle(self):
            @pl.loop(0, chunks)
            def _(c):
                for k in range(1, experts):
                    self.z_copy(c, k).wait_send()
                for m in range(chips):
                    self.g_copy(c, m).wait_send()
                for m in range(1, chips):
                    self.f_copy(c, m).wait_send()

            for k in range(experts):
                for m in range(chips):
                    self.h_copy(k, m).wait_send()
                for m in range(1, chips):
                    self.k_copy(k, m).wait_send()
                for m in range(members):
                    if k or m:
                        self.r_copy(k, m).wait_send()

    first, second = Part(0), Part(1)
    scale_copy().start()

    @pl.loop(0, chunks)
    def _(c):
        y_copy(c).start()

    scale_copy().wait_recv()
    scale[...] = jnp.broadcast_to(scale_in[0:1, :], (128, tokens)).T

    @pl.loop(0, chunks)
    def _(step):
        first.dispatch(step)

        def at(lag, stage):
            @pl.when(step >= lag)
            def _():
                stage(step - lag)

        at(LAG, second.dispatch)
        at(1, first.share)
        at(2, first.hand_on)

        @pl.when(step == 3)
        def _():
            for load in loads:
                load.wait()

        at(3, first.multiply)
        at(LAG + 1, second.share)
        at(LAG + 2, second.hand_on)
        at(LAG + 3, second.multiply)

    first.share(chunks - 1)
    pl.loop(chunks - LAG, chunks)(second.dispatch)
    first.hand_on(chunks - 2)
    first.multiply(chunks - 3)
    first.hand_on(chunks - 1)
    pl.loop(chunks - 2, chunks)(first.multiply)
    first.activate()
    pl.loop(chunks - LAG - 1, chunks - 1)(second.share)
    first.give_back()
    pl.loop(chunks - LAG - 2, chunks - 1)(second.hand_on)
    second.share(chunks - 1)
    pl.loop(chunks - LAG - 3, chunks - 1)(second.multiply)
    second.hand_on(chunks - 1)
    second.multiply(chunks - 1)
    second.activate()
    second.give_back()
    first.collect()
    for j in range(members):
        span = slice(j * width, (j + 1) * width)
        mid[:, span] = rows[:, span].astype(jnp.float32) + first.picked(j) * factor
    second.collect()
    for j in range(members):
        span = slice(j * width, (j + 1) * width)
        out[:, span] = (mid[:, span] + second.picked(j) * factor).astype(jnp.bfloat16)

    scale_copy().wait_send()

    @pl.loop(0, chunks)
    def _(c):
        y_copy(c).wait_send()

    first.settle()
    second.settle()


def per_device(sections, experts, members, prev_rows, expert_ids, route_weight, norm_gain, gate_weight, up_weight, down_weight):
    prev = prev_rows[0]
    tokens, feature = prev.shape
    capacity = 5 * tokens * expert_ids.shape[2] // (4 * experts)
    slots = -(-capacity // 8) * 8
    units, width = gate_weight.shape[3], down_weight.shape[3]
    chunks, chips = feature // CHUNK, members // 2
    bf16, f32 = jnp.bfloat16, jnp.float32
    dma = pltpu.SemaphoreType.DMA
    vmem, anywhere = pl.BlockSpec(memory_space=pltpu.VMEM), pl.BlockSpec(memory_space=pl.ANY)
    scratch = [
        pltpu.VMEM((tokens, feature), bf16),
        pltpu.VMEM((tokens, feature), bf16),
        pltpu.VMEM((8, tokens), f32),
        pltpu.VMEM((8, tokens), f32),
        pltpu.VMEM((tokens, 128), f32),
        pltpu.VMEM((tokens, feature), f32),
        pltpu.VMEM((feature, 2 * units), bf16),
        pltpu.VMEM((members * units, width), bf16),
        dma((3,)),
        dma((chunks + 1,)), dma((chunks + 1,)),
    ]
    for some in split(slots):
        lines = -(-(-(-width // 128) * some) // 16) * 16
        group = members * some
        padded = -(-(experts * some) // 128) * 128
        scratch += [
            pltpu.VMEM((padded, tokens), bf16),
            pltpu.VMEM((tokens, padded), bf16),
            pltpu.VMEM((chunks, experts, HALVES * some, CHUNK // HALVES), bf16),
            pltpu.VMEM((chunks, experts, members, HALVES * some, CHUNK // HALVES), bf16),
            pltpu.VMEM((experts * group, 2 * units), f32),
            pltpu.VMEM((experts, members, group, units), bf16),
            pltpu.VMEM((experts, members, lines, 128), bf16),
            pltpu.VMEM((experts, members, lines, 128), bf16),
            dma((chunks, experts)), dma((chunks, experts)),
            dma((chunks, chips)), dma((chunks, chips)),
            dma((chunks, chips)), dma((chunks, chips)),
            dma((experts, chips)), dma((experts, chips)),
            dma((experts, chips)), dma((experts, chips)),
            dma((experts, members)), dma((experts, members)),
        ]
    mixed = pl.pallas_call(
        functools.partial(kernel, sections, experts, members, slots),
        out_shape=jax.ShapeDtypeStruct((tokens, feature), bf16),
        in_specs=[vmem] * 4 + [anywhere] * 3,
        out_specs=vmem,
        scratch_shapes=scratch,
        compiler_params=pltpu.CompilerParams(
            collective_id=0, has_side_effects=True, vmem_limit_bytes=56 * 1024 * 1024
        ),
    )(
        prev, expert_ids[0].reshape(1, tokens), route_weight[0].reshape(1, tokens), norm_gain,
        gate_weight[0, 0], up_weight[0, 0], down_weight[0, 0],
    )
    return mixed[None]


def solution(mesh):
    placed = (
        P("section", ("node", "local"), None),
        P("section", ("node", "local"), None),
        P("section", ("node", "local"), None),
        P("section", None),
        P("section", "node", None, "local"),
        P("section", "node", None, "local"),
        P("section", "node", None, "local"),
    )
    sizes = mesh.shape
    return jax.shard_map(
        functools.partial(per_device, sizes["section"], sizes["node"], sizes["local"]),
        mesh=mesh,
        in_specs=placed,
        out_specs=P("section", ("node", "local"), None),
        check_vma=False,
    )
```

time: 187 us -> 83 us (0.44); the launches traced: 184 us -> 82.6 us
  Pallas kernels: 0 us -> 80.4 us
  blocking collectives: 78.7 us -> 0 us
  waiting for transfers between devices: 74.4 us -> 0 us
  between operations: 13.5 us -> 0.01 us
  matrix products: 11.2 us -> 0 us
  other arithmetic: 3.46 us -> 0 us
    pallas_call x0 -> x1, Pallas kernels: none -> 80.4 us  [per_device(): pl.pallas_call(functools.partial(kernel, sections, experts, members, slot...]
    all_to_all x3 -> x0, blocking collectives: 78.7 us -> none  [the longest x1 30 us: per_device(): lax.all_to_all(dispatched, 'node', split_axis=0, concat_axis=0, tiled=True)]
    all_gather x2 -> x0, waiting for transfers between devices: 57.3 us -> none  [the longest x1 38.8 us: per_device(): lax.all_gather(landed.reshape(-1, feature), 'local', axis=0, tiled=True)]
    ppermute x1 -> x0, waiting for transfers between devices: 17 us -> none  [passed_along(): lax.ppermute(value, axis, [(i, (i + by) % length) for i in range(length)])]
    dot_general x5 -> x0, matrix products: 11.2 us -> none  [the longest x1 4.37 us: per_device(): gate = jnp.dot(inputs, w_gate, preferred_element_type=jnp.float32)]
  transfers between devices with their start and end apart: 3 -> 0, of which waited for: 3 -> 0; matrix products, arithmetic and copies ran while one was open for 2% -> 0% of each run, Pallas kernels for 0% -> 0%
where the time goes in v2:
time: 83 us; the launch traced here: 82.6 us
  Pallas kernels  80.4 us (97%)
  local copies, waits for them, and re-layouts  2.16 us (3%)
    pallas_call x1, Pallas kernels, per_device(): pl.pallas_call(functools.partial(kernel, sections, experts, members, slot...  80.4 us
    unnamed x1, local copies, waits for them, and re-layouts  2.16 us

profile of v2, /device:TPU:9, one launch (start us, length us, event | category | flops | bytes accessed | tf_op | source)
XLA Modules:
  0.0 82.6 jit_solution(14913081465247568360)
XLA Ops:
  0.0 80.4 %shard_map.73 = bf16[128,3584]{1,0:T(8,128)(2,1)} custom-call(bf16[128,3584]{1,0:T(8,128)(2,1)} %bitcast.11, s32[1,128]{1,0:T(1,128)} %bitcast.12, f32[1,128]{1,0:T(1,128)} %bitcast.13, f32[1,3584]{1,0:T(1,128)} %gain.1, bf16[3584,256]{1,0:T(8,128)(2,1)} %bitcast.8, bf16[3584,256]{1,0:T(8,128)(2,1)} %bitcast.9, bf16[1024,896]{1,0:T(8,128)(2,1)} %bitcast.10), custom_call_target="tpu_custom_call" | custom-call | tf_op jit(solution)/shard_map/pallas_call | solution.py:367
  80.4 2.2 %copy.9 = bf16[1,128,3584]{2,1,0:T(8,128)(2,1)} copy(bf16[1,128,3584]{2,1,0:T(8,128)(2,1)} %bitcast.7) | data formatting | bytes 1835008

commit v3 on v2

--- a/solution.py
+++ b/solution.py
@@ -10,7 +10,8 @@
 MESH = pl.DeviceIdType.MESH
 HALVES = 2
 CHUNK = 512
-LAG = 3
+LAG = 4
+AHEAD = 3
 
 
 def split(slots):
@@ -140,7 +141,6 @@
 
         def dispatch(self, c):
             if self.p == 0:
-                y_copy(c).wait_recv()
                 normed = (
                     rows[:, columns(c)].astype(jnp.float32) * scale[:, 0:1] * gain[:, columns(c)]
                 ).astype(jnp.bfloat16)
@@ -192,12 +192,17 @@
                 for m in list(range(1, chips)) + [0]:
                     self.h_copy(k, m).start()
 
+        def pass_hidden(self, k):
+            for m in range(1, chips):
+                self.h_copy(k, m).wait_recv()
+                self.k_copy(k, m).start()
+
         def give_back(self):
-            for k in order:
+            self.pass_hidden(order[0])
+            for i, k in enumerate(order):
                 node = lax.rem(n + k, experts)
-                for m in range(1, chips):
-                    self.h_copy(k, m).wait_recv()
-                    self.k_copy(k, m).start()
+                if i + 1 < experts:
+                    self.pass_hidden(order[i + 1])
                 self.h_copy(k, 0).wait_recv()
                 for m in range(1, chips):
                     self.k_copy(k, m).wait_recv()
@@ -257,8 +262,7 @@
     first, second = Part(0), Part(1)
     scale_copy().start()
 
-    @pl.loop(0, chunks)
-    def _(c):
+    for c in range(AHEAD):
         y_copy(c).start()
 
     scale_copy().wait_recv()
@@ -266,6 +270,12 @@
 
     @pl.loop(0, chunks)
     def _(step):
+        y_copy(step).wait_recv()
+
+        @pl.when(step + AHEAD < chunks)
+        def _():
+            y_copy(step + AHEAD).start()
+
         first.dispatch(step)
 
         def at(lag, stage):
@@ -274,31 +284,35 @@
                 stage(step - lag)
 
         at(LAG, second.dispatch)
-        at(1, first.share)
-        at(2, first.hand_on)
-
-        @pl.when(step == 3)
+        at(2, first.share)
+        at(4, first.hand_on)
+
+        @pl.when(step == 5)
         def _():
             for load in loads:
                 load.wait()
 
-        at(3, first.multiply)
-        at(LAG + 1, second.share)
-        at(LAG + 2, second.hand_on)
-        at(LAG + 3, second.multiply)
-
+        at(5, first.multiply)
+        at(LAG + 2, second.share)
+
+    pl.loop(chunks - LAG, chunks - 2)(second.dispatch)
+    first.share(chunks - 2)
+    pl.loop(chunks - 2, chunks)(second.dispatch)
+    first.hand_on(chunks - 4)
+    first.multiply(chunks - 5)
+    first.hand_on(chunks - 3)
+    first.multiply(chunks - 4)
     first.share(chunks - 1)
-    pl.loop(chunks - LAG, chunks)(second.dispatch)
     first.hand_on(chunks - 2)
-    first.multiply(chunks - 3)
+    pl.loop(chunks - 3, chunks - 1)(first.multiply)
     first.hand_on(chunks - 1)
-    pl.loop(chunks - 2, chunks)(first.multiply)
+    first.multiply(chunks - 1)
     first.activate()
-    pl.loop(chunks - LAG - 1, chunks - 1)(second.share)
+    pl.loop(chunks - LAG - 2, chunks - 1)(second.share)
     first.give_back()
-    pl.loop(chunks - LAG - 2, chunks - 1)(second.hand_on)
     second.share(chunks - 1)
-    pl.loop(chunks - LAG - 3, chunks - 1)(second.multiply)
+    pl.loop(0, chunks - 1)(second.hand_on)
+    pl.loop(0, chunks - 1)(second.multiply)
     second.hand_on(chunks - 1)
     second.multiply(chunks - 1)
     second.activate()

time: 83 us -> 88.3 us (1.064)
  Pallas kernels: 80.4 us -> 85.5 us
    pallas_call x1, Pallas kernels: 80.4 us -> 85.5 us  [per_device(): pl.pallas_call(functools.partial(kernel, sections, experts, members, slot...]
where the time goes in v3:
time: 88.3 us; the launch traced here: 87.7 us
  Pallas kernels  85.5 us (97%)
  local copies, waits for them, and re-layouts  2.16 us (2%)
    pallas_call x1, Pallas kernels, per_device(): pl.pallas_call(functools.partial(kernel, sections, experts, members, slot...  85.5 us
    unnamed x1, local copies, waits for them, and re-layouts  2.16 us

profile of v3, /device:TPU:9, one launch (start us, length us, event | category | flops | bytes accessed | tf_op | source)
XLA Modules:
  0.0 87.7 jit_solution(14189372523418311186)
XLA Ops:
  0.0 85.5 %shard_map.73 = bf16[128,3584]{1,0:T(8,128)(2,1)} custom-call(bf16[128,3584]{1,0:T(8,128)(2,1)} %bitcast.11, s32[1,128]{1,0:T(1,128)} %bitcast.12, f32[1,128]{1,0:T(1,128)} %bitcast.13, f32[1,3584]{1,0:T(1,128)} %gain.1, bf16[3584,256]{1,0:T(8,128)(2,1)} %bitcast.8, bf16[3584,256]{1,0:T(8,128)(2,1)} %bitcast.9, bf16[1024,896]{1,0:T(8,128)(2,1)} %bitcast.10), custom_call_target="tpu_custom_call" | custom-call | tf_op jit(solution)/shard_map/pallas_call | solution.py:381
  85.5 2.2 %copy.9 = bf16[1,128,3584]{2,1,0:T(8,128)(2,1)} copy(bf16[1,128,3584]{2,1,0:T(8,128)(2,1)} %bitcast.7) | data formatting | bytes 1835008

commit v4 on v3

--- a/solution.py
+++ b/solution.py
@@ -10,8 +10,6 @@
 MESH = pl.DeviceIdType.MESH
 HALVES = 2
 CHUNK = 512
-LAG = 4
-AHEAD = 3
 
 
 def split(slots):
@@ -20,9 +18,9 @@
 
 
 def kernel(sections, experts, members, slots, prev, ids, weight, gain, w_gate, w_up, w_down, out, *scratch):
-    rows, normal, scale_out, scale_in, scale, mid, w_in, w_out, w_sem, y_send, y_recv = scratch[:11]
-    own = (len(scratch) - 11) // 2
-    parts = [scratch[11 : 11 + own], scratch[11 + own :]]
+    rows, normal, ids_in, gain_in, mid, w_in, w_out, w_sem, y_send, y_recv = scratch[:10]
+    own = (len(scratch) - 10) // 2
+    parts = [scratch[10 : 10 + own], scratch[10 + own :]]
     s, n, l = lax.axis_index("section"), lax.axis_index("node"), lax.axis_index("local")
     tokens, feature = prev.shape
     chunks = feature // CHUNK
@@ -45,41 +43,46 @@
 
     barrier = pltpu.get_barrier_semaphore()
     after, before = lax.rem(s + 1, sections), lax.rem(s + sections - 1, sections)
-    for other in (after, before):
-        pl.semaphore_signal(barrier, inc=1, device_id={"section": other, "node": n, "local": l}, device_id_type=MESH)
+    pl.semaphore_signal(barrier, inc=1, device_id={"section": after, "node": n, "local": l}, device_id_type=MESH)
     for k in range(experts):
+        node = lax.rem(n + k, experts)
+        pl.semaphore_signal(barrier, inc=1, device_id={"section": before, "node": node, "local": l}, device_id_type=MESH)
         for m in range(members):
             if k or m:
-                place = {"section": s, "node": lax.rem(n + k, experts), "local": lax.rem(l + m, members)}
+                place = {"section": s, "node": node, "local": lax.rem(l + m, members)}
                 pl.semaphore_signal(barrier, inc=1, device_id=place, device_id_type=MESH)
 
+    pool = split(slots)
+
+    def spreads(row):
+        chosen = jnp.broadcast_to(row.astype(jnp.float32), (128, tokens)).T
+        lanes = lax.broadcasted_iota(jnp.int32, (tokens, 128), 1).astype(jnp.float32)
+        onehot = jnp.where(chosen == lanes, 1.0, 0.0)
+        earlier = lax.broadcasted_iota(jnp.int32, (tokens, tokens), 1) < lax.broadcasted_iota(
+            jnp.int32, (tokens, tokens), 0
+        )
+        counts = jnp.dot(
+            jnp.where(earlier, 1.0, 0.0).astype(jnp.bfloat16), onehot.astype(jnp.bfloat16),
+            preferred_element_type=jnp.float32,
+        )
+        slot = jnp.sum(counts * onehot, axis=1, keepdims=True)
+        made = []
+        for p in range(2):
+            local_slot = slot - (pool[0] if p else 0)
+            inside = jnp.logical_and(local_slot >= 0, local_slot < pool[p])
+            target = jnp.where(inside, chosen[:, 0:1] * pool[p] + local_slot, -1.0)
+            places = lax.broadcasted_iota(jnp.int32, (tokens, parts[p][0].shape[0]), 1).astype(jnp.float32)
+            made.append(jnp.where(target == places, 1.0, 0.0))
+        return made
+
+    for p, spread in enumerate(spreads(ids[...])):
+        parts[p][1][...] = spread.astype(jnp.bfloat16)
+        parts[p][4][...] = jnp.zeros_like(parts[p][4])
     wide = prev[...].astype(jnp.float32)
-    mean = jnp.sum(wide * wide, axis=1, keepdims=True) / feature
-    scale_out[...] = jnp.broadcast_to(lax.rsqrt(mean + 1e-06), (tokens, 128)).T[0:8, :]
-
-    chosen = jnp.broadcast_to(ids[...].astype(jnp.float32), (128, tokens)).T
-    lanes = lax.broadcasted_iota(jnp.int32, (tokens, 128), 1).astype(jnp.float32)
-    onehot = jnp.where(chosen == lanes, 1.0, 0.0)
-    earlier = lax.broadcasted_iota(jnp.int32, (tokens, tokens), 1) < lax.broadcasted_iota(jnp.int32, (tokens, tokens), 0)
-    counts = jnp.dot(
-        jnp.where(earlier, 1.0, 0.0).astype(jnp.bfloat16), onehot.astype(jnp.bfloat16),
-        preferred_element_type=jnp.float32,
-    )
-    slot = jnp.sum(counts * onehot, axis=1, keepdims=True)
-    pool = split(slots)
-    for p in range(2):
-        sel, sel_t, total = parts[p][0], parts[p][1], parts[p][4]
-        local_slot = slot - (pool[0] if p else 0)
-        inside = jnp.logical_and(local_slot >= 0, local_slot < pool[p])
-        target = jnp.where(inside, chosen[:, 0:1] * pool[p] + local_slot, -1.0)
-        places = lax.broadcasted_iota(jnp.int32, (tokens, sel.shape[0]), 1).astype(jnp.float32)
-        spread = jnp.where(target == places, 1.0, 0.0)
-        sel_t[...] = spread.astype(jnp.bfloat16)
-        sel[...] = spread.T.astype(jnp.bfloat16)
-        total[...] = jnp.zeros_like(total)
+    scale = lax.rsqrt(jnp.sum(wide * wide, axis=1, keepdims=True) / feature + 1e-06)
     factor = jnp.broadcast_to(weight[...], (128, tokens)).T[:, 0:1]
 
-    pl.semaphore_wait(barrier, experts * members + 1)
+    pl.semaphore_wait(barrier, experts * members + experts)
 
     def remote(src, dst, send, recv, **place):
         where = {"section": s, "node": n, "local": l}
@@ -91,11 +94,14 @@
     def columns(c):
         return pl.ds(pl.multiple_of(c * CHUNK, CHUNK), CHUNK)
 
-    def scale_copy():
-        return remote(scale_out, scale_in, y_send.at[chunks], y_recv.at[chunks], section=after)
-
-    def y_copy(c):
-        return remote(prev.at[:, columns(c)], rows.at[:, columns(c)], y_send.at[c], y_recv.at[c], section=after)
+    def ids_copy():
+        return remote(ids, ids_in, y_send.at[0], y_recv.at[0], section=before)
+
+    def gain_copy():
+        return remote(gain, gain_in, y_send.at[1], y_recv.at[1], section=before)
+
+    def rows_copy():
+        return remote(prev, rows, y_send.at[2], y_recv.at[2], section=after)
 
     class Part:
         def __init__(self, p):
@@ -106,10 +112,9 @@
 
         def z_copy(self, c, k):
             node = lax.rem(n + k, experts)
-            if k == 0:
-                return pltpu.make_async_copy(self.packed.at[c, n], self.arrived.at[c, n, l], self.z_recv.at[c, 0])
             return remote(
-                self.packed.at[c, node], self.arrived.at[c, n, l], self.z_send.at[c, k], self.z_recv.at[c, k], node=node
+                self.packed.at[c, node], self.arrived.at[c, n, l], self.z_send.at[c, k], self.z_recv.at[c, k],
+                section=after, node=node,
             )
 
         def g_copy(self, c, m):
@@ -142,7 +147,7 @@
         def dispatch(self, c):
             if self.p == 0:
                 normed = (
-                    rows[:, columns(c)].astype(jnp.float32) * scale[:, 0:1] * gain[:, columns(c)]
+                    prev[:, columns(c)].astype(jnp.float32) * scale * gain_in[:, columns(c)]
                 ).astype(jnp.bfloat16)
                 normal[:, columns(c)] = normed
             else:
@@ -159,8 +164,7 @@
                 self.z_copy(c, k).start()
 
         def share(self, c):
-            self.z_copy(c, 0).wait()
-            for k in range(1, experts):
+            for k in range(experts):
                 self.z_copy(c, k).wait_recv()
             for m in list(range(1, chips)) + [0]:
                 self.g_copy(c, m).start()
@@ -197,24 +201,20 @@
                 self.h_copy(k, m).wait_recv()
                 self.k_copy(k, m).start()
 
-        def give_back(self):
-            self.pass_hidden(order[0])
-            for i, k in enumerate(order):
-                node = lax.rem(n + k, experts)
-                if i + 1 < experts:
-                    self.pass_hidden(order[i + 1])
-                self.h_copy(k, 0).wait_recv()
-                for m in range(1, chips):
-                    self.k_copy(k, m).wait_recv()
-                inner = jnp.concatenate([self.hidden[node, j] for j in range(members)], axis=1)
-                made = jnp.dot(inner, w_out[...], preferred_element_type=jnp.float32)
-                for j in range(members):
-                    for t in range(tiles):
-                        self.results[node, j, t * self.slots : (t + 1) * self.slots, 0 : ends[t]] = made[
-                            j * self.slots : (j + 1) * self.slots, t * 128 : t * 128 + ends[t]
-                        ].astype(jnp.bfloat16)
-                for m in range(members):
-                    self.r_copy(k, m).start()
+        def give_back(self, k):
+            node = lax.rem(n + k, experts)
+            self.h_copy(k, 0).wait_recv()
+            for m in range(1, chips):
+                self.k_copy(k, m).wait_recv()
+            inner = jnp.concatenate([self.hidden[node, j] for j in range(members)], axis=1)
+            made = jnp.dot(inner, w_out[...], preferred_element_type=jnp.float32)
+            for j in range(members):
+                for t in range(tiles):
+                    self.results[node, j, t * self.slots : (t + 1) * self.slots, 0 : ends[t]] = made[
+                        j * self.slots : (j + 1) * self.slots, t * 128 : t * 128 + ends[t]
+                    ].astype(jnp.bfloat16)
+            for m in range(members):
+                self.r_copy(k, m).start()
 
         def collect(self):
             for k in order:
@@ -243,7 +243,7 @@
         def settle(self):
             @pl.loop(0, chunks)
             def _(c):
-                for k in range(1, experts):
+                for k in range(experts):
                     self.z_copy(c, k).wait_send()
                 for m in range(chips):
                     self.g_copy(c, m).wait_send()
@@ -260,63 +260,62 @@
                         self.r_copy(k, m).wait_send()
 
     first, second = Part(0), Part(1)
-    scale_copy().start()
-
-    for c in range(AHEAD):
-        y_copy(c).start()
-
-    scale_copy().wait_recv()
-    scale[...] = jnp.broadcast_to(scale_in[0:1, :], (128, tokens)).T
+    ids_copy().start()
+    gain_copy().start()
+    ids_copy().wait_recv()
+    for p, spread in enumerate(spreads(ids_in[...])):
+        parts[p][0][...] = spread.T.astype(jnp.bfloat16)
+    gain_copy().wait_recv()
+
+    pl.loop(0, chunks)(first.dispatch)
 
     @pl.loop(0, chunks)
     def _(step):
-        y_copy(step).wait_recv()
-
-        @pl.when(step + AHEAD < chunks)
+        second.dispatch(step)
+        first.share(step)
+
+        @pl.when(step >= 1)
         def _():
-            y_copy(step + AHEAD).start()
-
-        first.dispatch(step)
-
-        def at(lag, stage):
-            @pl.when(step >= lag)
-            def _():
-                stage(step - lag)
-
-        at(LAG, second.dispatch)
-        at(2, first.share)
-        at(4, first.hand_on)
-
-        @pl.when(step == 5)
+            first.hand_on(step - 1)
+
+        @pl.when(step == 2)
         def _():
             for load in loads:
                 load.wait()
 
-        at(5, first.multiply)
-        at(LAG + 2, second.share)
-
-    pl.loop(chunks - LAG, chunks - 2)(second.dispatch)
-    first.share(chunks - 2)
-    pl.loop(chunks - 2, chunks)(second.dispatch)
-    first.hand_on(chunks - 4)
-    first.multiply(chunks - 5)
-    first.hand_on(chunks - 3)
-    first.multiply(chunks - 4)
-    first.share(chunks - 1)
-    first.hand_on(chunks - 2)
-    pl.loop(chunks - 3, chunks - 1)(first.multiply)
+        @pl.when(step >= 2)
+        def _():
+            first.multiply(step - 2)
+
+    early = chunks // 3
+    later = 2 * early
+    pl.loop(0, early)(second.share)
     first.hand_on(chunks - 1)
+    first.multiply(chunks - 2)
+    pl.loop(early, later)(second.share)
     first.multiply(chunks - 1)
     first.activate()
-    pl.loop(chunks - LAG - 2, chunks - 1)(second.share)
-    first.give_back()
-    second.share(chunks - 1)
-    pl.loop(0, chunks - 1)(second.hand_on)
-    pl.loop(0, chunks - 1)(second.multiply)
-    second.hand_on(chunks - 1)
-    second.multiply(chunks - 1)
+    rows_copy().start()
+    pl.loop(later, chunks - 1)(second.share)
+    pl.loop(0, later)(second.hand_on)
+    for i, k in enumerate(order):
+        first.pass_hidden(k)
+        if i == 0:
+            second.share(chunks - 1)
+        if i:
+            first.give_back(order[i - 1])
+        pl.loop(i * later // experts, (i + 1) * later // experts)(second.multiply)
+        if i == experts - 2:
+            pl.loop(later, chunks)(second.hand_on)
+    first.give_back(order[-1])
+    pl.loop(later, chunks)(second.multiply)
     second.activate()
-    second.give_back()
+    second.pass_hidden(order[0])
+    for i, k in enumerate(order):
+        if i + 1 < experts:
+            second.pass_hidden(order[i + 1])
+        second.give_back(k)
+    rows_copy().wait_recv()
     first.collect()
     for j in range(members):
         span = slice(j * width, (j + 1) * width)
@@ -326,12 +325,9 @@
         span = slice(j * width, (j + 1) * width)
         out[:, span] = (mid[:, span] + second.picked(j) * factor).astype(jnp.bfloat16)
 
-    scale_copy().wait_send()
-
-    @pl.loop(0, chunks)
-    def _(c):
-        y_copy(c).wait_send()
-
+    ids_copy().wait_send()
+    gain_copy().wait_send()
+    rows_copy().wait_send()
     first.settle()
     second.settle()
 
@@ -349,14 +345,13 @@
     scratch = [
         pltpu.VMEM((tokens, feature), bf16),
         pltpu.VMEM((tokens, feature), bf16),
-        pltpu.VMEM((8, tokens), f32),
-        pltpu.VMEM((8, tokens), f32),
-        pltpu.VMEM((tokens, 128), f32),
+        pltpu.VMEM((1, tokens), jnp.int32),
+        pltpu.VMEM((1, feature), f32),
         pltpu.VMEM((tokens, feature), f32),
         pltpu.VMEM((feature, 2 * units), bf16),
         pltpu.VMEM((members * units, width), bf16),
         dma((3,)),
-        dma((chunks + 1,)), dma((chunks + 1,)),
+        dma((3,)), dma((3,)),
     ]
     for some in split(slots):
         lines = -(-(-(-width // 128) * some) // 16) * 16

time: 88.3 us -> 80.5 us (0.912)
  Pallas kernels: 85.5 us -> 77.7 us
    pallas_call x1, Pallas kernels: 85.5 us -> 77.7 us  [per_device(): pl.pallas_call(functools.partial(kernel, sections, experts, members, slot...]
where the time goes in v4:
time: 80.5 us; the launch traced here: 79.9 us
  Pallas kernels  77.7 us (97%)
  local copies, waits for them, and re-layouts  2.16 us (3%)
    pallas_call x1, Pallas kernels, per_device(): pl.pallas_call(functools.partial(kernel, sections, experts, members, slot...  77.7 us
    unnamed x1, local copies, waits for them, and re-layouts  2.16 us

profile of v4, /device:TPU:9, one launch (start us, length us, event | category | flops | bytes accessed | tf_op | source)
XLA Modules:
  0.0 79.9 jit_solution(18226448945368821960)
XLA Ops:
  0.0 77.7 %shard_map.73 = bf16[128,3584]{1,0:T(8,128)(2,1)} custom-call(bf16[128,3584]{1,0:T(8,128)(2,1)} %bitcast.11, s32[1,128]{1,0:T(1,128)} %bitcast.12, f32[1,128]{1,0:T(1,128)} %bitcast.13, f32[1,3584]{1,0:T(1,128)} %gain.1, bf16[3584,256]{1,0:T(8,128)(2,1)} %bitcast.8, bf16[3584,256]{1,0:T(8,128)(2,1)} %bitcast.9, bf16[1024,896]{1,0:T(8,128)(2,1)} %bitcast.10), custom_call_target="tpu_custom_call" | custom-call | tf_op jit(solution)/shard_map/pallas_call | solution.py:376
  77.7 2.2 %copy.9 = bf16[1,128,3584]{2,1,0:T(8,128)(2,1)} copy(bf16[1,128,3584]{2,1,0:T(8,128)(2,1)} %bitcast.7) | data formatting | bytes 1835008

commit v5 on v4

--- a/solution.py
+++ b/solution.py
@@ -9,6 +9,7 @@
 
 MESH = pl.DeviceIdType.MESH
 HALVES = 2
+FLYING = 3
 CHUNK = 512
 
 
@@ -267,36 +268,53 @@
         parts[p][0][...] = spread.T.astype(jnp.bfloat16)
     gain_copy().wait_recv()
 
-    pl.loop(0, chunks)(first.dispatch)
+    pl.loop(0, FLYING)(first.dispatch)
 
     @pl.loop(0, chunks)
     def _(step):
-        second.dispatch(step)
         first.share(step)
 
-        @pl.when(step >= 1)
-        def _():
-            first.hand_on(step - 1)
-
-        @pl.when(step == 2)
+        @pl.when(step + FLYING < chunks)
+        def _():
+            first.dispatch(step + FLYING)
+
+        @pl.when(step + FLYING >= chunks)
+        def _():
+            second.dispatch(step + FLYING - chunks)
+
+        @pl.when(step >= 2)
+        def _():
+            first.hand_on(step - 2)
+
+        @pl.when(step == 3)
         def _():
             for load in loads:
                 load.wait()
 
-        @pl.when(step >= 2)
-        def _():
-            first.multiply(step - 2)
+        @pl.when(step >= 3)
+        def _():
+            first.multiply(step - 3)
+
+    def move(c):
+        second.share(c)
+
+        @pl.when(c + FLYING + 1 < chunks)
+        def _():
+            second.dispatch(c + FLYING + 1)
 
     early = chunks // 3
     later = 2 * early
-    pl.loop(0, early)(second.share)
+    second.dispatch(FLYING)
+    first.hand_on(chunks - 2)
+    first.multiply(chunks - 3)
+    pl.loop(0, early)(move)
     first.hand_on(chunks - 1)
     first.multiply(chunks - 2)
-    pl.loop(early, later)(second.share)
+    pl.loop(early, early + 1)(move)
     first.multiply(chunks - 1)
     first.activate()
+    pl.loop(early + 1, chunks - 1)(move)
     rows_copy().start()
-    pl.loop(later, chunks - 1)(second.share)
     pl.loop(0, later)(second.hand_on)
     for i, k in enumerate(order):
         first.pass_hidden(k)

time: 80.5 us -> 76.8 us (0.954)
  Pallas kernels: 77.7 us -> 74.2 us
    pallas_call x1, Pallas kernels: 77.7 us -> 74.2 us  [per_device(): pl.pallas_call(functools.partial(kernel, sections, experts, members, slot...]
where the time goes in v5:
time: 76.8 us; the launch traced here: 76.4 us
  Pallas kernels  74.2 us (97%)
  local copies, waits for them, and re-layouts  2.16 us (3%)
    pallas_call x1, Pallas kernels, per_device(): pl.pallas_call(functools.partial(kernel, sections, experts, members, slot...  74.2 us
    unnamed x1, local copies, waits for them, and re-layouts  2.16 us

profile of v5, /device:TPU:9, one launch (start us, length us, event | category | flops | bytes accessed | tf_op | source)
XLA Modules:
  0.0 76.4 jit_solution(13996933916449923443)
XLA Ops:
  0.0 74.2 %shard_map.73 = bf16[128,3584]{1,0:T(8,128)(2,1)} custom-call(bf16[128,3584]{1,0:T(8,128)(2,1)} %bitcast.11, s32[1,128]{1,0:T(1,128)} %bitcast.12, f32[1,128]{1,0:T(1,128)} %bitcast.13, f32[1,3584]{1,0:T(1,128)} %gain.1, bf16[3584,256]{1,0:T(8,128)(2,1)} %bitcast.8, bf16[3584,256]{1,0:T(8,128)(2,1)} %bitcast.9, bf16[1024,896]{1,0:T(8,128)(2,1)} %bitcast.10), custom_call_target="tpu_custom_call" | custom-call | tf_op jit(solution)/shard_map/pallas_call | solution.py:394
  74.2 2.2 %copy.9 = bf16[1,128,3584]{2,1,0:T(8,128)(2,1)} copy(bf16[1,128,3584]{2,1,0:T(8,128)(2,1)} %bitcast.7) | data formatting | bytes 1835008
